TPU v7x, 512 devices: a whole 4x4x16 slice. The times are simulated.
512 devices in a mesh: freq: 32 (over y, x, core), src: 2 (over z_hi), rcv: 8 (over z_lo).
Axes of the slice: x: 4, y: 4, z: 16 (z_hi: 2, z_lo: 8; z = z_hi * 8 + z_lo), core: 2. Of those that a mesh axis runs over, the one named last changes fastest.
Arguments:
- packets: bfloat16 [1048576, 256], P(('freq', 'src', 'rcv')), parts along dimension 0, may hold values from -6 to 6
- packet_bin: int32 [1048576], P(('freq', 'src', 'rcv')), parts along dimension 0, may hold values from 0 to 32767, as said below
- obliquity: bfloat16 [65536], P(('freq', 'src')), parts along dimension 0, may hold values from 0.0066223145 to 0.06591797
- wavelet: float32 [64], P('freq'), parts along dimension 0, may hold values from 0.5 to 1.5
Outputs:
- multiples: float32 [2, 65536, 2048], P(None, ('freq', 'src'), 'rcv'), parts along dimension 1
There are 32 independent parts, one for each index of `freq`. A program takes and returns all parts, laid end to end along the dimension named above; each array names one. Nothing has to cross between parts.
Inputs may be any that keep to these rules, and one draw needn't show every extreme that they name: `packet_bin`: within one part every bin id appears exactly once over all devices' lists. The owner of bin s * 16 + c is the device with src index s // (2048 // 2) and rcv index c // (2048 // 8 // 128). One device's list holds at most 256 bins of any one owner; every device holds exactly 256 bins of one owner, and every owner receives exactly 256 bins from one device.
All inputs are finite; a program needn't handle non-finite values.
Results may differ from a plain program's by a relative error of at most 0.0029.
Values may be sent and summed in bfloat16 or wider, within the bound.
A program may use at most 64 MiB of HBM per device.

v0:
```python
import jax
import jax.numpy as jnp
from jax import lax
from jax.sharding import PartitionSpec as P

N = 2048


def complex_product(left_factor, right_factor):
    product_real = jnp.dot(
        left_factor[0], right_factor[0], preferred_element_type=jnp.float32
    ) - jnp.dot(left_factor[1], right_factor[1], preferred_element_type=jnp.float32)
    product_imag = jnp.dot(
        left_factor[0], right_factor[1], preferred_element_type=jnp.float32
    ) + jnp.dot(left_factor[1], right_factor[0], preferred_element_type=jnp.float32)
    return jnp.stack([product_real, product_imag])


def apply_filter(data_block, weights, wavelet):
    real_part = data_block[0].astype(jnp.float32)
    imag_part = data_block[1].astype(jnp.float32)
    obl_scale = weights.astype(jnp.float32)[:, None]
    filt_real = (wavelet[0] * real_part - wavelet[1] * imag_part) * obl_scale
    filt_imag = (wavelet[0] * imag_part + wavelet[1] * real_part) * obl_scale
    return jnp.stack([filt_real, filt_imag]).astype(jnp.bfloat16)


def on_device(packets, packet_bin, obliquity, wavelet):
    src_count = lax.axis_size("src")
    rcv_count = lax.axis_size("rcv")
    grid_size = src_count * rcv_count
    per_device = packets.shape[0]
    row_width = packets.shape[1]
    block_len = row_width // 2
    capacity = 2 * per_device // grid_size
    rows_dev = obliquity.shape[0]
    cols_dev = N // rcv_count
    blocks_dev = cols_dev // block_len
    total_blocks = N // block_len
    source = packet_bin // total_blocks
    recv_block = packet_bin % total_blocks
    owner_id = source // rows_dev * rcv_count + recv_block // blocks_dev
    local_slot = source % rows_dev * blocks_dev + recv_block % blocks_dev
    one_hot = (owner_id[:, None] == jnp.arange(grid_size, dtype=jnp.int32)[None, :]).astype(
        jnp.int32
    )
    slot_rank = jnp.sum(jnp.cumsum(one_hot, axis=0) * one_hot, axis=1) - 1
    send_slot = owner_id * capacity + slot_rank
    send_rows = (
        jnp.zeros((grid_size * capacity, row_width), jnp.bfloat16).at[send_slot].set(packets)
    )
    send_index = jnp.full((grid_size * capacity,), -1, jnp.int32).at[send_slot].set(local_slot)
    recv_rows, recv_index = (
        lax.all_to_all(
            send_rows.reshape(grid_size, capacity, row_width),
            ("src", "rcv"),
            split_axis=0,
            concat_axis=0,
            tiled=True,
        ),
        lax.all_to_all(
            send_index.reshape(grid_size, capacity),
            ("src", "rcv"),
            split_axis=0,
            concat_axis=0,
            tiled=True,
        ),
    )
    target = jnp.where(recv_index >= 0, recv_index, per_device).reshape(-1)
    binned = (
        jnp.zeros((per_device, row_width), jnp.bfloat16)
        .at[target]
        .set(recv_rows.reshape(-1, row_width), mode="drop")
    )
    data_block = (
        binned.reshape(rows_dev, blocks_dev, 2, block_len)
        .transpose(2, 0, 1, 3)
        .reshape(2, rows_dev, cols_dev)
    )
    left_panel = lax.all_gather(data_block, "rcv", axis=2, tiled=True)
    filtered = apply_filter(data_block, obliquity, wavelet)
    return complex_product(left_panel, lax.all_gather(filtered, "src", axis=1, tiled=True))


def solution(mesh):
    return jax.shard_map(
        on_device,
        mesh=mesh,
        in_specs=(
            P(("freq", "src", "rcv"), None),
            P(("freq", "src", "rcv")),
            P(("freq", "src")),
            P("freq"),
        ),
        out_specs=P(None, ("freq", "src"), "rcv"),
        check_vma=False,
    )
```

profile of v0, /device:TPU:1, one launch (start us, length us, event | category | flops | bytes accessed | tf_op | source)
XLA Modules:
  0.0 495.4 jit_solution(9061913617330983162)
XLA Ops:
  6.5 0.7 fusion.22
  7.3 4.5 reduce-window.6
  11.8 0.4 slice_reduce_fusion
  12.3 0.2 reduce-window.9
  12.4 0.1 broadcast_add_fusion
  12.5 0.1 fusion.17
  12.6 8.6 %scatter_custom_fusion = s32[4096]{0:T(1024)} fusion(s32[2048]{0:T(1024)S(1)} %compare_select_fusion.2, s32[2048]{0:T(1024)S(1)} %get-tuple-element.7, s32[]{:T(128)} %constant.76.clone.1), kind=kCustom, calls=%fused_computation.65 | custom fusion | bytes 16388 | tf_op jit(solution)/shard_map/scatter | solution.py:52
  21.2 15.7 %all-to-all-start = ((s32[16,1,256]{2,1,0:T(1,128)}), s32[16,1,256]{2,1,0:T(1,128)S(1)}, u32[]{:S(2)}, u32[]{:S(2)}) async-start(s32[16,1,256]{2,1,0:T(1,128)} %bitcast.2), calls=%async_computation | async-start | bytes 32768 | tf_op jit(solution)/shard_map/all_to_all | solution.py:61
  37.0 11.3 %scatter_custom_fusion.1 = bf16[4096,256]{1,0:T(8,128)(2,1)} fusion(s32[2048]{0:T(1024)S(1)} %compare_select_fusion.2, bf16[2048,256]{1,0:T(8,128)(2,1)} %param.4, bf16[]{:T(256)} %constant.75.clone.1), kind=kCustom, calls=%fused_computation.28 | custom fusion | bytes 2097664 | tf_op jit(solution)/shard_map/scatter | solution.py:50
  48.2 0.1 all-to-all-done
  48.4 0.0 copy-start.1
  48.4 0.0 copy-start.2
  48.4 11.5 %all-to-all-start.1 = ((bf16[16,256,256]{2,1,0:T(8,128)(2,1)}), bf16[16,256,256]{2,1,0:T(8,128)(2,1)S(1)}, u32[]{:S(2)}, u32[]{:S(2)}) async-start(bf16[16,256,256]{2,1,0:T(8,128)(2,1)} %bitcast.5), calls=%async_computation.1 | async-start | bytes 4194304 | tf_op jit(solution)/shard_map/all_to_all | solution.py:54
  59.9 0.0 all-gather.5.cloned.1.call-start
  59.9 0.0 copy-done.1
  59.9 0.0 copy-done.2
  59.9 0.6 fusion.31
  60.6 91.1 %all-to-all-done.1 = bf16[16,256,256]{2,1,0:T(8,128)(2,1)S(1)} async-done(((bf16[16,256,256]{2,1,0:T(8,128)(2,1)}), bf16[16,256,256]{2,1,0:T(8,128)(2,1)S(1)}, u32[]{:S(2)}, u32[]{:S(2)}) %all-to-all-start.1) | async-done | bytes 2097184 | tf_op jit(solution)/shard_map/all_to_all | solution.py:54
  151.7 0.0 copy-start
  151.7 1.3 copy-done
  153.0 18.4 %scatter_custom_fusion.2 = bf16[2048,256]{1,0:T(8,128)(2,1)S(1)} fusion(s32[4096]{0:T(1024)S(1)} %bitcast.74, bf16[4096,256]{1,0:T(8,128)(2,1)} %bitcast.69, bf16[]{:T(256)} %constant.75.clone.1), kind=kCustom, calls=%fused_computation.30 | custom fusion | bytes 1049088 | tf_op jit(solution)/shard_map/scatter | solution.py:73
  171.5 0.3 reshape.167
  171.8 0.1 copy.16
  171.9 2.5 fusion.8
  174.4 1.6 copy.10
  176.0 1.3 copy.11
  177.3 1.5 fusion.11
  178.8 1.1 pad_maximum_fusion.1
  179.9 0.0 all-gather.5.cloned.1.call-update
  179.9 0.2 all-gather.3.cloned.1.call-start
  180.1 2.5 copy.12
  182.6 0.0 all-gather.3.cloned.1.call-update
  182.6 108.8 %all-gather.5.cloned.1.call-done = bf16[2,2048,256]{1,2,0:T(8,128)(2,1)} async-done(((bf16[2,1024,256]{1,2,0:T(8,128)(2,1)}), bf16[2,2048,256]{1,2,0:T(8,128)(2,1)}) %all-gather.5.cloned.1.call-update) | async-done | bytes 2097168 | tf_op jit(solution)/shard_map/all_gather | solution.py:82
  291.4 185.3 %all-gather.3.cloned.1.call-done = bf16[2,1024,2048]{1,2,0:T(8,128)(2,1)} async-done(((bf16[2,1024,256]{1,2,0:T(8,128)(2,1)}), bf16[2,1024,2048]{1,2,0:T(8,128)(2,1)}) %all-gather.3.cloned.1.call-update) | async-done | bytes 8388624 | tf_op jit(solution)/shard_map/all_gather | solution.py:80
  476.7 0.0 copy-start.3
  476.7 3.9 fusion
  480.7 1.0 copy-done.3
  481.7 0.0 copy-start.4
  481.7 2.7 fusion.1
  484.4 0.0 copy-done.4
  484.4 1.3 fusion.7
  485.7 1.3 fusion.5
  487.1 1.5 pad_maximum_fusion
  (4 shorter events, 0.0 us)
Async XLA Ops:
  21.2 27.1 %all-to-all-start = ((s32[16,1,256]{2,1,0:T(1,128)}), s32[16,1,256]{2,1,0:T(1,128)S(1)}, u32[]{:S(2)}, u32[]{:S(2)}) async-start(s32[16,1,256]{2,1,0:T(1,128)} %bitcast.2), calls=%async_computation | async-start | bytes 32768 | tf_op jit(solution)/shard_map/all_to_all | solution.py:61
  48.4 11.5 %copy-start.1 = (bf16[1024]{0:T(1024)(128)(2,1)S(1)}, bf16[1024]{0:T(1024)(128)(2,1)}, u32[]{:S(2)}) copy-start(bf16[1024]{0:T(1024)(128)(2,1)} %param.6) | copy-start | bytes 6148
  48.4 11.5 %copy-start.2 = (f32[2]{0:T(128)S(1)}, f32[2]{0:T(128)}, u32[]{:S(2)}) copy-start(f32[2]{0:T(128)} %param.7) | copy-start | bytes 28
  48.4 103.3 %all-to-all-start.1 = ((bf16[16,256,256]{2,1,0:T(8,128)(2,1)}), bf16[16,256,256]{2,1,0:T(8,128)(2,1)S(1)}, u32[]{:S(2)}, u32[]{:S(2)}) async-start(bf16[16,256,256]{2,1,0:T(8,128)(2,1)} %bitcast.5), calls=%async_computation.1 | async-start | bytes 4194304 | tf_op jit(solution)/shard_map/all_to_all | solution.py:54
  59.9 231.5 %all-gather.5.cloned.1.call-start = ((), (), s32[]{:S(2)}) async-start(), calls=%async_computation.3 | async-start | bytes 3145728 | tf_op jit(solution)/shard_map/all_gather | solution.py:82
  151.7 1.3 copy-start
  179.9 296.9 %all-gather.3.cloned.1.call-start = ((), (), s32[]{:S(2)}) async-start(), calls=%async_computation.2 | async-start | bytes 9437184 | tf_op jit(solution)/shard_map/all_gather | solution.py:80
  476.7 5.0 copy-start.3
  481.7 2.7 copy-start.4
Sparse Core Ops, SparseCore 0:
  180.0 111.3 all-gather.4
  293.5 183.2 all-gather.2
where the time goes:
time: 496 us; the launch traced here: 495 us
  waiting for transfers between devices  385 us (78%)
  local copies, waits for them, and re-layouts  47.5 us (10%)
  starting transfers between devices  27.5 us (6%)
  between operations  13.6 us (3%)
  other arithmetic  12.2 us (2%)
  matrix products  9.27 us (2%)
    all_gather x1, waiting for transfers between devices, on_device(): left_panel = lax.all_gather(data_block, 'rcv', axis=2, tiled=True)  185 us
    all_gather x1, waiting for transfers between devices, on_device(): lax.all_gather(filtered, 'src', axis=1, tiled=True)  109 us
    all_to_all x1, waiting for transfers between devices, on_device(): lax.all_to_all(send_rows.reshape(grid_size, capacity, row_width), ('src',...  91.1 us
    scatter x1, local copies, waits for them, and re-layouts, on_device(): binned = jnp.zeros((per_device, row_width), jnp.bfloat16).at[target].set(...  18.4 us
    all_to_all x1, starting transfers between devices, on_device(): lax.all_to_all(send_index.reshape(grid_size, capacity), ('src', 'rcv'), s...  15.7 us
    all_to_all x1, starting transfers between devices, on_device(): lax.all_to_all(send_rows.reshape(grid_size, capacity, row_width), ('src',...  11.5 us
    scatter x1, local copies, waits for them, and re-layouts, on_device(): jnp.zeros((grid_size * capacity, row_width), jnp.bfloat16).at[send_slot]  11.3 us
  transfers between devices with their start and end apart: 4, of which 4 were waited for; matrix products, arithmetic and copies ran while one was open for 3% of the time, Pallas kernels for 0%

commit v1 on v0

v1 whole, which is shorter than its diff:
```python
import functools

import jax
import jax.numpy as jnp
from jax import lax
from jax.experimental import pallas as pl
from jax.experimental.pallas import tpu as pltpu
from jax.sharding import PartitionSpec as P

MESH = pl.DeviceIdType.MESH
N = 2048
RB = 128
BLOCKS = N // RB
GROUP = 16
HALF = N // 2
PK = 2048
WIDTH = 2 * RB
SUB = 4
ROWS = PK // SUB
FAR = GROUP // 2
WIN = 384
PANELS = BLOCKS + 2
BF16 = jnp.bfloat16
F32 = jnp.float32


def kernel(rows_ref, bins_ref, obl_in_ref, wave_ref, out_ref, *scratch):
    bufs, scratch = scratch[:16], scratch[16:]
    auxs, scratch = scratch[:16], scratch[16:]
    tabs, scratch = scratch[:16], scratch[16:]
    (panel, weights, onehot, key_cols, key_rows, rank_rows, digits, obl, send_sem, recv_sem,
     aux_send, aux_recv, tab_sem, obl_sem) = scratch

    src, rcv = lax.axis_index("src"), lax.axis_index("rcv")
    me = src * (GROUP // 2) + rcv

    def device(rank):
        rank = lax.rem(rank + GROUP, GROUP)
        return {"src": rank // (GROUP // 2), "rcv": lax.rem(rank, GROUP // 2)}

    ahead = (device(me + 1), device(me - 1))
    partner = device(me + FAR)

    def place(d, t):
        if t == 0:
            return 0
        if t == FAR:
            return 15
        return t if d == 0 else t + 7

    def carried(d, t, s):
        return t < FAR - 1 or (s < SUB // 2) == (d == 0)

    def data_copy(d, t, s):
        part = pl.ds(s * ROWS, ROWS)
        return pltpu.make_async_remote_copy(
            src_ref=bufs[place(d, t)].at[part],
            dst_ref=bufs[place(d, t + 1)].at[part],
            send_sem=send_sem.at[d, t, s],
            recv_sem=recv_sem.at[d, t, s],
            device_id=ahead[d],
            device_id_type=MESH,
        )

    def aux_copy(d, t):
        return pltpu.make_async_remote_copy(
            src_ref=auxs[place(d, t)],
            dst_ref=auxs[place(d, t + 1)],
            send_sem=aux_send.at[d, t],
            recv_sem=aux_recv.at[d, t],
            device_id=ahead[d],
            device_id_type=MESH,
        )

    def table_copy(i):
        return pltpu.make_async_copy(auxs[i].at[pl.ds(16, 8)], tabs[i], tab_sem.at[i])

    obl_copy = pltpu.make_async_remote_copy(
        src_ref=obl.at[0],
        dst_ref=obl.at[1],
        send_sem=obl_sem.at[0],
        recv_sem=obl_sem.at[1],
        device_id=partner,
        device_id_type=MESH,
    )

    barrier = pltpu.get_barrier_semaphore()
    for other in (*ahead, partner):
        pl.semaphore_signal(barrier, inc=1, device_id=other, device_id_type=MESH)

    bins = bins_ref[...]
    keys = ((bins >> 14) << 14) + ((bins & 15) << 10) + ((bins >> 4) & 1023)
    key_rows[...] = keys
    digits[...] = jnp.zeros_like(digits)
    high, low = (keys >> 7).astype(F32), (keys & 127).astype(F32)
    for i in range(BLOCKS):
        lanes = slice(i * RB, (i + 1) * RB)
        digits[0:1, lanes] = high[i : i + 1, :]
        digits[1:2, lanes] = low[i : i + 1, :]
        key_cols[i * RB : (i + 1) * RB, :] = jnp.broadcast_to(key_rows[i : i + 1, :], (RB, RB)).T

    def rank_block(i, _):
        mine = jnp.broadcast_to(key_rows[pl.ds(i, 1), :], (RB, RB))
        total = jnp.zeros((RB, RB), jnp.int32)
        for j in range(BLOCKS):
            total += jnp.where(key_cols[j * RB : (j + 1) * RB, :] < mine, 1, 0)
        rank_rows[pl.ds(i, 1), :] = jnp.sum(total, axis=0, keepdims=True)
        return 0

    lax.fori_loop(0, BLOCKS, rank_block, 0)
    obl[0] = obl_in_ref[...]
    pl.semaphore_wait(barrier, 3)
    obl_copy.start()

    two_digits = digits[...].astype(BF16)
    for s in range(SUB):
        slots = lax.broadcasted_iota(jnp.int32, (ROWS, RB), 0) + s * ROWS
        for i in range(BLOCKS):
            onehot[:, i * RB : (i + 1) * RB] = jnp.where(
                slots == rank_rows[i : i + 1, :], 1.0, 0.0
            ).astype(BF16)
        taken = onehot[...]
        bufs[0][s * ROWS : (s + 1) * ROWS, :] = jnp.dot(
            taken, rows_ref[...], preferred_element_type=F32
        ).astype(BF16)
        for d in (0, 1):
            data_copy(d, 0, s).start()
        found = lax.dot_general(
            two_digits, taken, (((1,), (1,)), ((), ())), preferred_element_type=F32
        )
        found = (found[0:1, :] * 128.0 + found[1:2, :]).astype(jnp.int32)
        per = ROWS // RB
        for i in range(per):
            auxs[0][s * per + i : s * per + i + 1, :] = found[:, i * RB : (i + 1) * RB]
    starts = lax.broadcasted_iota(jnp.int32, (RB, RB), 1) * HALF
    total = jnp.zeros((RB, RB), jnp.int32)
    for j in range(BLOCKS):
        total += jnp.where(key_cols[j * RB : (j + 1) * RB, :] < starts, 1, 0)
    offsets = jnp.sum(total, axis=0, keepdims=True)
    auxs[0][16:24, :] = jnp.broadcast_to(offsets, (8, RB))
    for d in (0, 1):
        aux_copy(d, 0).start()
    table_copy(0).start()
    table_copy(0).wait()

    slot_ids = lax.broadcasted_iota(jnp.int32, (HALF, RB), 0)

    def bucket(lists, first, j, _):
        b = jnp.where(j < BLOCKS, src * BLOCKS + j, (1 - src) * BLOCKS + rcv * 2 + j - BLOCKS)
        hits, packets = [], []
        for i in lists:
            k = jnp.clip(tabs[i][0, b] // RB, 0, (PK - WIN) // RB)
            for w in range(WIN // RB):
                ids = auxs[i][pl.ds(k + w, 1), :] - b * HALF
                hits.append(jnp.where(slot_ids == ids, 1.0, 0.0).astype(BF16))
            packets.append(bufs[i][pl.ds(k * RB, WIN), :])
        taken = jnp.concatenate(hits, axis=1)
        found = packets[0] if len(packets) == 1 else jnp.concatenate(packets, axis=0)
        placed = jnp.dot(taken, found, preferred_element_type=F32).astype(BF16)
        lanes = pl.ds(pl.multiple_of(j * WIDTH, WIDTH), WIDTH)
        if first:
            panel[:, lanes] = placed
        else:
            panel[:, lanes] += placed
        return 0

    def buckets(lists, first, low, high):
        lax.fori_loop(low, high, functools.partial(bucket, lists, first), 0)

    edges = [PANELS * s // SUB for s in range(SUB + 1)]
    for t in range(FAR):
        lists = (0,) if t == 0 else (place(0, t), place(1, t))
        for s in range(SUB):
            for d in (0, 1):
                if carried(d, t, s):
                    data_copy(d, t, s).wait_recv()
                    if t + 1 < FAR and carried(d, t + 1, s):
                        data_copy(d, t + 1, s).start()
            if s == SUB - 1:
                for d in (0, 1):
                    if t + 1 < FAR or d == 0:
                        aux_copy(d, t).wait_recv()
                        i = place(d, t + 1)
                        table_copy(i).start()
                        if t + 2 < FAR or (t + 2 == FAR and d == 0):
                            aux_copy(d, t + 1).start()
                for d in (0, 1):
                    if t + 1 < FAR or d == 0:
                        table_copy(place(d, t + 1)).wait()
            buckets(lists, t == 0, edges[s], edges[s + 1])
    buckets((15,), False, 0, PANELS)

    obl_copy.wait()
    w0, w1 = wave_ref[0], wave_ref[1]

    def filter_block(c, _):
        here = c // (BLOCKS // 2) == src
        lane = jnp.where(here, rcv * 2 * WIDTH, BLOCKS * WIDTH)
        block = lax.rem(c, BLOCKS // 2)
        data = panel[
            pl.ds(pl.multiple_of(block * RB, RB), RB),
            pl.ds(pl.multiple_of(lane, 2 * WIDTH), 2 * WIDTH),
        ].astype(F32)
        row = obl[jnp.where(here, 0, 1), pl.ds(block, 1), :]
        scale = jnp.broadcast_to(row, (RB, RB)).T
        for i in range(2):
            re = data[:, i * WIDTH : i * WIDTH + RB]
            im = data[:, i * WIDTH + RB : (i + 1) * WIDTH]
            filt_re = ((w0 * re - w1 * im) * scale).astype(BF16)
            filt_im = ((w0 * im + w1 * re) * scale).astype(BF16)
            k = pl.multiple_of(c * WIDTH, WIDTH)
            left, right = slice(i * RB, (i + 1) * RB), slice(WIDTH + i * RB, WIDTH + (i + 1) * RB)
            weights[pl.ds(k, RB), left] = filt_re
            weights[pl.ds(k, RB), right] = filt_im
            weights[pl.ds(k + RB, RB), left] = -filt_im
            weights[pl.ds(k + RB, RB), right] = filt_re
        return 0

    lax.fori_loop(0, BLOCKS, filter_block, 0)

    tile = 512

    def product(m, _):
        part = pl.ds(pl.multiple_of(m * tile, tile), tile)
        for i in range(2):
            out_ref[i, part, :] = jnp.dot(
                panel[part, : BLOCKS * WIDTH],
                weights[:, i * WIDTH : (i + 1) * WIDTH],
                preferred_element_type=F32,
            )
        return 0

    lax.fori_loop(0, HALF // tile, product, 0)

    for t in range(FAR):
        for d in (0, 1):
            for s in range(SUB):
                if carried(d, t, s):
                    data_copy(d, t, s).wait_send()
            if t + 1 < FAR or d == 0:
                aux_copy(d, t).wait_send()


def on_device(packets, packet_bin, obliquity, wavelet):
    vmem = pl.BlockSpec(memory_space=pltpu.VMEM)
    dma = pltpu.SemaphoreType.DMA
    return pl.pallas_call(
        kernel,
        out_shape=jax.ShapeDtypeStruct((2, HALF, WIDTH), F32),
        in_specs=[vmem, vmem, vmem, pl.BlockSpec(memory_space=pltpu.SMEM)],
        out_specs=vmem,
        scratch_shapes=[
            *[pltpu.VMEM((PK, WIDTH), BF16)] * 16,
            *[pltpu.VMEM((24, RB), jnp.int32)] * 16,
            *[pltpu.SMEM((8, RB), jnp.int32)] * 16,
            pltpu.VMEM((HALF, PANELS * WIDTH), BF16),
            pltpu.VMEM((BLOCKS * WIDTH, 2 * WIDTH), BF16),
            pltpu.VMEM((ROWS, PK), BF16),
            pltpu.VMEM((PK, RB), jnp.int32),
            pltpu.VMEM((BLOCKS, RB), jnp.int32),
            pltpu.VMEM((BLOCKS, RB), jnp.int32),
            pltpu.VMEM((8, PK), F32),
            pltpu.VMEM((2, 8, RB), F32),
            dma((2, FAR, SUB)),
            dma((2, FAR, SUB)),
            dma((2, FAR)),
            dma((2, FAR)),
            dma((16,)),
            dma((2,)),
        ],
        compiler_params=pltpu.CompilerParams(
            collective_id=0, has_side_effects=True, vmem_limit_bytes=56 << 20
        ),
    )(
        packets,
        packet_bin.reshape(BLOCKS, RB),
        obliquity.astype(F32).reshape(8, RB),
        wavelet,
    )


def solution(mesh):
    return jax.shard_map(
        on_device,
        mesh=mesh,
        in_specs=(
            P(("freq", "src", "rcv"), None),
            P(("freq", "src", "rcv")),
            P(("freq", "src")),
            P("freq"),
        ),
        out_specs=P(None, ("freq", "src"), "rcv"),
        check_vma=False,
    )
```

time: 496 us -> 219 us (0.44)
  waiting for transfers between devices: 385 us -> 0 us
  Pallas kernels: 0 us -> 215 us
  local copies, waits for them, and re-layouts: 47.5 us -> 3.05 us
  starting transfers between devices: 27.5 us -> 0 us
  between operations: 13.6 us -> 0.01 us
  other arithmetic: 12.2 us -> 1.27 us
  matrix products: 9.27 us -> 0 us
    all_gather x2 -> x0, waiting for transfers between devices: 294 us -> none  [the longest x1 185 us: on_device(): left_panel = lax.all_gather(data_block, 'rcv', axis=2, tiled=True)]
    pallas_call x0 -> x1, Pallas kernels: none -> 215 us  [on_device(): pl.pallas_call(kernel, out_shape=jax.ShapeDtypeStruct((2, HALF, WIDTH), F...]
    all_to_all x2 -> x0, waiting for transfers between devices: 91.2 us -> none  [the longest x1 91.1 us: on_device(): lax.all_to_all(send_rows.reshape(grid_size, capacity, row_width), ('src',...]
    scatter x3 -> x0, local copies, waits for them, and re-layouts: 38.3 us -> none  [the longest x1 18.4 us: on_device(): binned = jnp.zeros((per_device, row_width), jnp.bfloat16).at[target].set(...]
    all_to_all x2 -> x0, starting transfers between devices: 27.2 us -> none  [the longest x1 15.7 us: on_device(): lax.all_to_all(send_index.reshape(grid_size, capacity), ('src', 'rcv'), s...]
    dot_general x4 -> x0, matrix products: 9.27 us -> none  [the longest x1 3.94 us: complex_product(): jnp.dot(left_factor[0], right_factor[1], preferred_element_type=jnp.float32)]
    another operation x6 -> x0, other arithmetic: 8.84 us -> none
  transfers between devices with their start and end apart: 4 -> 0, of which waited for: 4 -> 0; matrix products, arithmetic and copies ran while one was open for 3% -> 0% of each run, Pallas kernels for 0% -> 0%
where the time goes in v1:
time: 219 us
  Pallas kernels  215 us (98%)
  local copies, waits for them, and re-layouts  3.05 us (1%)
    pallas_call x1, Pallas kernels, on_device(): pl.pallas_call(kernel, out_shape=jax.ShapeDtypeStruct((2, HALF, WIDTH), F...  215 us

profile of v1, /device:TPU:1, one launch (start us, length us, event | category | flops | bytes accessed | tf_op | source)
XLA Modules:
  0.0 219.1 jit_solution(6865148929543239482)
XLA Ops:
  0.0 1.3 bitcast_convert_fusion.obl_in_ref
  1.3 214.8 %shard_map.46 = f32[2,1024,256]{2,1,0:T(8,128)} custom-call(bf16[2048,256]{1,0:T(8,128)(2,1)} %rows_ref.1, s32[16,128]{1,0:T(8,128)} %bitcast.4, f32[8,128]{1,0:T(8,128)} %bitcast_convert_fusion.obl_in_ref, f32[2]{0:T(128)} %wave_ref.1), custom_call_target="tpu_custom_call" | custom-call | tf_op jit(solution)/shard_map/pallas_call | solution.py:247
  216.1 3.0 %copy.6 = f32[2,1024,256]{2,1,0:T(8,128)} copy(f32[2,1024,256]{2,1,0:T(8,128)} %shard_map.46) | data formatting | bytes 4194304

commit v2 on v1

v2 whole, which is shorter than its diff:
```python
import functools

import jax
import jax.numpy as jnp
from jax import lax
from jax.experimental import pallas as pl
from jax.experimental.pallas import tpu as pltpu
from jax.sharding import PartitionSpec as P

MESH = pl.DeviceIdType.MESH
N = 2048
RB = 128
BLOCKS = N // RB
GROUP = 16
HALF = N // 2
PK = 2048
WIDTH = 2 * RB
SUB = 4
ROWS = PK // SUB
FAR = GROUP // 2
WIN = 384
PANELS = BLOCKS + 2
PAIR, ONE = 3, 6
BF16 = jnp.bfloat16
F32 = jnp.float32


def kernel(rows_ref, bins_ref, obl_in_ref, wave_ref, out_ref, lists, auxs, tabs, now, now_aux, panel, weights,
           slots16, onehot, key_cols, key_rows, rank_rows, digits, obl, send_sem, recv_sem, aux_send, aux_recv,
           obl_send, obl_recv, tab_sem):
    src, rcv = lax.axis_index("src"), lax.axis_index("rcv")
    me = src * FAR + rcv

    def device(rank):
        rank = lax.rem(rank + GROUP, GROUP)
        return {"src": rank // FAR, "rcv": lax.rem(rank, FAR)}

    ahead = (device(me + 1), device(me - 1))

    def place(d, t):
        if d == 0:
            return t
        if isinstance(t, int):
            return t if t in (0, FAR) else t + FAR
        return jnp.where(lax.rem(t, FAR) == 0, t, t + FAR)

    def data_copy(d, t, s):
        part = pl.ds(s * ROWS, ROWS)
        return pltpu.make_async_remote_copy(
            src_ref=lists.at[place(d, t), part],
            dst_ref=lists.at[place(d, t + 1), part],
            send_sem=send_sem.at[d, t, s],
            recv_sem=recv_sem.at[d, t, s],
            device_id=ahead[d],
            device_id_type=MESH,
        )

    def aux_copy(d, t):
        return pltpu.make_async_remote_copy(
            src_ref=auxs.at[place(d, t)],
            dst_ref=auxs.at[place(d, t + 1)],
            send_sem=aux_send.at[d, t],
            recv_sem=aux_recv.at[d, t],
            device_id=ahead[d],
            device_id_type=MESH,
        )

    def obl_copy(t):
        return pltpu.make_async_remote_copy(
            src_ref=obl.at[t],
            dst_ref=obl.at[t + 1],
            send_sem=obl_send.at[t],
            recv_sem=obl_recv.at[t],
            device_id=ahead[0],
            device_id_type=MESH,
        )

    def table_copy(i):
        return pltpu.make_async_copy(auxs.at[i, pl.ds(BLOCKS, 8)], tabs.at[i], tab_sem.at[i])

    barrier = pltpu.get_barrier_semaphore()
    for other in ahead:
        pl.semaphore_signal(barrier, inc=1, device_id=other, device_id_type=MESH)

    bins = bins_ref[...]
    keys = ((bins >> 14) << 14) + ((bins & 15) << 10) + ((bins >> 4) & 1023)
    key_rows[...] = keys
    digits[...] = jnp.zeros_like(digits)
    high, low = (keys >> 7).astype(F32), (keys & 127).astype(F32)
    for i in range(BLOCKS):
        lanes = slice(i * RB, (i + 1) * RB)
        digits[0:1, lanes] = high[i : i + 1, :]
        digits[1:2, lanes] = low[i : i + 1, :]
        key_cols[i * RB : (i + 1) * RB, :] = jnp.broadcast_to(key_rows[i : i + 1, :], (RB, RB)).T

    def rank_block(i, _):
        mine = jnp.broadcast_to(key_rows[pl.ds(i, 1), :], (RB, RB))
        total = jnp.zeros((RB, RB), jnp.int32)
        for j in range(BLOCKS):
            total += jnp.where(key_cols[j * RB : (j + 1) * RB, :] < mine, 1, 0)
        rank_rows[pl.ds(i, 1), :] = jnp.sum(total, axis=0, keepdims=True)
        return 0

    lax.fori_loop(0, BLOCKS, rank_block, 0)
    obl[0] = obl_in_ref[...]
    pl.semaphore_wait(barrier, 2)

    two_digits = digits[...].astype(BF16)
    for s in range(SUB):
        slots = lax.broadcasted_iota(jnp.int32, (ROWS, RB), 0) + s * ROWS
        for i in range(BLOCKS):
            onehot[:, i * RB : (i + 1) * RB] = jnp.where(
                slots == rank_rows[i : i + 1, :], 1.0, 0.0
            ).astype(BF16)
        taken = onehot[...]
        lists[0, s * ROWS : (s + 1) * ROWS, :] = jnp.dot(
            taken, rows_ref[...], preferred_element_type=F32
        ).astype(BF16)
        for d in (0, 1):
            data_copy(d, 0, s).start()
        found = lax.dot_general(
            two_digits, taken, (((1,), (1,)), ((), ())), preferred_element_type=F32
        )
        found = (found[0:1, :] * 128.0 + found[1:2, :]).astype(jnp.int32)
        per = ROWS // RB
        for i in range(per):
            auxs[0, s * per + i : s * per + i + 1, :] = found[:, i * RB : (i + 1) * RB]
    starts = lax.broadcasted_iota(jnp.int32, (RB, RB), 1) * HALF
    total = jnp.zeros((RB, RB), jnp.int32)
    for j in range(BLOCKS):
        total += jnp.where(key_cols[j * RB : (j + 1) * RB, :] < starts, 1, 0)
    offsets = jnp.sum(total, axis=0, keepdims=True)
    auxs[0, BLOCKS:, :] = jnp.broadcast_to(offsets, (8, RB))
    for d in (0, 1):
        aux_copy(d, 0).start()
    obl_copy(0).start()
    table_copy(0).start()
    table_copy(0).wait()

    slot_ids = lax.broadcasted_iota(jnp.int32, (HALF // 16, 16, RB), 0) * 16
    slot_ids = (slot_ids + lax.broadcasted_iota(jnp.int32, (HALF // 16, 16, RB), 1)).astype(jnp.int16)
    slots16[...] = slot_ids
    panel[...] = jnp.zeros_like(panel)

    def take(i, slot):
        def some(r, _):
            part = pl.ds(r * WIDTH, WIDTH)
            now[i, part, :] = lists[slot, part, :]
            return 0

        lax.fori_loop(0, PK // WIDTH, some, 0)
        now_aux[i] = auxs[slot, :BLOCKS, :]

    def place_rows(slots, count, g, _):
        placed = []
        for j in [g * count + i for i in range(count)]:
            b = jnp.where(j < BLOCKS, src * BLOCKS + j, (1 - src) * BLOCKS + rcv * 2 + j - BLOCKS)
            hits, packets = [], []
            for i, slot in enumerate(slots):
                k = jnp.clip(tabs[slot, 0, b] // RB, 0, (PK - WIN) // RB)
                for w in range(WIN // RB):
                    ids = now_aux[i, pl.ds(k + w, 1), :] - b * HALF
                    ids = jnp.broadcast_to(ids, (16, RB)).astype(jnp.int16)
                    hit = jnp.where(slots16[...] == ids[None], jnp.ones((), BF16), jnp.zeros((), BF16))
                    hits.append(hit.reshape(HALF, RB))
                packets.append(now[i, pl.ds(k * RB, WIN), :])
            found = packets[0] if len(packets) == 1 else jnp.concatenate(packets, axis=0)
            placed.append(
                jnp.dot(jnp.concatenate(hits, axis=1), found, preferred_element_type=F32).astype(BF16)
            )
        lanes = pl.ds(pl.multiple_of(g * (count * WIDTH), count * WIDTH), count * WIDTH)
        panel[:, lanes] += jnp.concatenate(placed, axis=1)
        return 0

    def step(t, _):
        slots = (t, place(1, t))
        take(0, slots[0])
        take(1, slots[1])

        @pl.when(t == 0)
        def _():
            now_aux[1] = jnp.full((BLOCKS, RB), -1, jnp.int32)

        def sub_block(s, _):
            groups = PANELS // PAIR
            lax.fori_loop(
                groups * s // SUB, groups * (s + 1) // SUB, functools.partial(place_rows, slots, PAIR), 0
            )

            @pl.when(t < FAR - 1)
            def _():
                for d in (0, 1):
                    data_copy(d, t, s).wait_recv()

                    @pl.when((t < FAR - 2) | ((s < SUB // 2) == (d == 0)))
                    def _(d=d):
                        data_copy(d, t + 1, s).start()

            return 0

        lax.fori_loop(0, SUB, sub_block, 0)

        @pl.when(t < FAR - 1)
        def _():
            for d in (0, 1):
                aux_copy(d, t).wait_recv()
                table_copy(place(d, t + 1)).start()
            aux_copy(0, t + 1).start()

            @pl.when(t < FAR - 2)
            def _():
                aux_copy(1, t + 1).start()

            obl_copy(t).wait_recv()
            obl_copy(t + 1).start()
            for d in (0, 1):
                table_copy(place(d, t + 1)).wait()

        return 0

    lax.fori_loop(0, FAR, step, 0)
    aux_copy(0, FAR - 1).wait_recv()
    table_copy(FAR).start()
    for s in range(SUB):
        data_copy(int(s >= SUB // 2), FAR - 1, s).wait_recv()
    take(0, FAR)
    table_copy(FAR).wait()
    lax.fori_loop(0, PANELS // ONE, functools.partial(place_rows, (FAR,), ONE), 0)

    obl_copy(FAR - 1).wait_recv()
    w0, w1 = wave_ref[0], wave_ref[1]

    def filter_block(c, _):
        here = c // (BLOCKS // 2) == src
        lane = jnp.where(here, rcv * 2 * WIDTH, BLOCKS * WIDTH)
        block = lax.rem(c, BLOCKS // 2)
        data = panel[
            pl.ds(pl.multiple_of(block * RB, RB), RB),
            pl.ds(pl.multiple_of(lane, 2 * WIDTH), 2 * WIDTH),
        ].astype(F32)
        row = obl[jnp.where(here, 0, FAR), pl.ds(block, 1), :]
        scale = jnp.broadcast_to(row, (RB, RB)).T
        for i in range(2):
            re = data[:, i * WIDTH : i * WIDTH + RB]
            im = data[:, i * WIDTH + RB : (i + 1) * WIDTH]
            filt_re = ((w0 * re - w1 * im) * scale).astype(BF16)
            filt_im = ((w0 * im + w1 * re) * scale).astype(BF16)
            k = pl.multiple_of(c * WIDTH, WIDTH)
            left, right = slice(i * RB, (i + 1) * RB), slice(WIDTH + i * RB, WIDTH + (i + 1) * RB)
            weights[pl.ds(k, RB), left] = filt_re
            weights[pl.ds(k, RB), right] = filt_im
            weights[pl.ds(k + RB, RB), left] = -filt_im
            weights[pl.ds(k + RB, RB), right] = filt_re
        return 0

    lax.fori_loop(0, BLOCKS, filter_block, 0)

    tile = 512

    def product(m, _):
        part = pl.ds(pl.multiple_of(m * tile, tile), tile)
        for i in range(2):
            out_ref[i, part, :] = jnp.dot(
                panel[part, : BLOCKS * WIDTH],
                weights[:, i * WIDTH : (i + 1) * WIDTH],
                preferred_element_type=F32,
            )
        return 0

    lax.fori_loop(0, HALF // tile, product, 0)

    def sent(t, _):
        for d in (0, 1):
            for s in range(SUB):

                @pl.when((t < FAR - 1) | ((s < SUB // 2) == (d == 0)))
                def _(d=d, s=s):
                    data_copy(d, t, s).wait_send()

        aux_copy(0, t).wait_send()
        obl_copy(t).wait_send()

        @pl.when(t < FAR - 1)
        def _():
            aux_copy(1, t).wait_send()

        return 0

    lax.fori_loop(0, FAR, sent, 0)


def on_device(packets, packet_bin, obliquity, wavelet):
    vmem = pl.BlockSpec(memory_space=pltpu.VMEM)
    dma = pltpu.SemaphoreType.DMA
    return pl.pallas_call(
        kernel,
        out_shape=jax.ShapeDtypeStruct((2, HALF, WIDTH), F32),
        in_specs=[vmem, vmem, vmem, pl.BlockSpec(memory_space=pltpu.SMEM)],
        out_specs=vmem,
        scratch_shapes=[
            pltpu.VMEM((GROUP, PK, WIDTH), BF16),
            pltpu.VMEM((GROUP, 24, RB), jnp.int32),
            pltpu.SMEM((GROUP, 8, RB), jnp.int32),
            pltpu.VMEM((2, PK, WIDTH), BF16),
            pltpu.VMEM((2, BLOCKS, RB), jnp.int32),
            pltpu.VMEM((HALF, PANELS * WIDTH), BF16),
            pltpu.VMEM((BLOCKS * WIDTH, 2 * WIDTH), BF16),
            pltpu.VMEM((HALF // 16, 16, RB), jnp.int16),
            pltpu.VMEM((ROWS, PK), BF16),
            pltpu.VMEM((PK, RB), jnp.int32),
            pltpu.VMEM((BLOCKS, RB), jnp.int32),
            pltpu.VMEM((BLOCKS, RB), jnp.int32),
            pltpu.VMEM((8, PK), F32),
            pltpu.VMEM((FAR + 1, 8, RB), F32),
            dma((2, FAR, SUB)),
            dma((2, FAR, SUB)),
            dma((2, FAR)),
            dma((2, FAR)),
            dma((FAR,)),
            dma((FAR,)),
            dma((GROUP,)),
        ],
        compiler_params=pltpu.CompilerParams(
            collective_id=0, has_side_effects=True, vmem_limit_bytes=46 << 20
        ),
    )(
        packets,
        packet_bin.reshape(BLOCKS, RB),
        obliquity.astype(F32).reshape(8, RB),
        wavelet,
    )


def solution(mesh):
    return jax.shard_map(
        on_device,
        mesh=mesh,
        in_specs=(
            P(("freq", "src", "rcv"), None),
            P(("freq", "src", "rcv")),
            P(("freq", "src")),
            P("freq"),
        ),
        out_specs=P(None, ("freq", "src"), "rcv"),
        check_vma=False,
    )
```

time: 219 us -> 206 us (0.941)
  Pallas kernels: 215 us -> 201 us
    pallas_call x1, Pallas kernels: 215 us -> 201 us  [on_device(): pl.pallas_call(kernel, out_shape=jax.ShapeDtypeStruct((2, HALF, WIDTH), F...]
where the time goes in v2:
time: 206 us
  Pallas kernels  201 us (98%)
  local copies, waits for them, and re-layouts  3.9 us (2%)
    pallas_call x1, Pallas kernels, on_device(): pl.pallas_call(kernel, out_shape=jax.ShapeDtypeStruct((2, HALF, WIDTH), F...  201 us

profile of v2, /device:TPU:1, one launch (start us, length us, event | category | flops | bytes accessed | tf_op | source)
XLA Modules:
  0.0 205.8 jit_solution(11464126848671515798)
XLA Ops:
  0.0 0.7 bitcast_convert_fusion.obl_in_ref
  0.7 0.0 copy-start
  0.7 1.2 copy-done
  1.9 0.0 copy-start.1
  1.9 0.7 copy-done.1
  2.6 0.0 copy-start.2
  2.6 0.7 copy-done.2
  3.3 201.2 %shard_map.46 = f32[2,1024,256]{2,1,0:T(8,128)S(1)} custom-call(bf16[2048,256]{1,0:T(8,128)(2,1)S(1)} %copy-done, s32[16,128]{1,0:T(8,128)S(1)} %bitcast.4, f32[8,128]{1,0:T(8,128)S(1)} %bitcast_convert_fusion.obl_in_ref, f32[2]{0:T(128)S(1)} %copy-done.2), custom_call_target="tpu_custom_call" | custom-call | tf_op jit(solution)/shard_map/pallas_call | solution.py:295
  204.4 1.3 copy.6
Async XLA Ops:
  0.7 1.2 copy-start
  1.9 0.7 copy-start.1
  2.6 0.7 copy-start.2

commit v3 on v2

--- a/solution.py
+++ b/solution.py
@@ -25,9 +25,14 @@
 F32 = jnp.float32
 
 
-def kernel(rows_ref, bins_ref, obl_in_ref, wave_ref, out_ref, lists, auxs, tabs, now, now_aux, panel, weights,
-           slots16, onehot, key_cols, key_rows, rank_rows, digits, obl, send_sem, recv_sem, aux_send, aux_recv,
-           obl_send, obl_recv, tab_sem):
+def kernel(rows_hbm, bins_hbm, obl_in_ref, wave_hbm, out_ref, rows_ref, bins_ref, wave_ref, lists, auxs, offs, tabs,
+           now, now_aux, panel, weights, slots16, onehot, key_cols, key_rows, rank_rows, digits, obl, send_sem,
+           recv_sem, aux_send, aux_recv, off_send, off_recv, obl_send, obl_recv, tab_sem, in_sem):
+    bins_in = pltpu.make_async_copy(bins_hbm, bins_ref, in_sem.at[0])
+    rows_in = pltpu.make_async_copy(rows_hbm, rows_ref, in_sem.at[1])
+    wave_in = pltpu.make_async_copy(wave_hbm, wave_ref, in_sem.at[2])
+    for copy in (bins_in, rows_in, wave_in):
+        copy.start()
     src, rcv = lax.axis_index("src"), lax.axis_index("rcv")
     me = src * FAR + rcv
 
@@ -65,6 +70,16 @@
             device_id_type=MESH,
         )
 
+    def off_copy(d, t):
+        return pltpu.make_async_remote_copy(
+            src_ref=offs.at[place(d, t)],
+            dst_ref=offs.at[place(d, t + 1)],
+            send_sem=off_send.at[d, t],
+            recv_sem=off_recv.at[d, t],
+            device_id=ahead[d],
+            device_id_type=MESH,
+        )
+
     def obl_copy(t):
         return pltpu.make_async_remote_copy(
             src_ref=obl.at[t],
@@ -76,12 +91,13 @@
         )
 
     def table_copy(i):
-        return pltpu.make_async_copy(auxs.at[i, pl.ds(BLOCKS, 8)], tabs.at[i], tab_sem.at[i])
+        return pltpu.make_async_copy(offs.at[i], tabs.at[i], tab_sem.at[i])
 
     barrier = pltpu.get_barrier_semaphore()
     for other in ahead:
         pl.semaphore_signal(barrier, inc=1, device_id=other, device_id_type=MESH)
 
+    bins_in.wait()
     bins = bins_ref[...]
     keys = ((bins >> 14) << 14) + ((bins & 15) << 10) + ((bins >> 4) & 1023)
     key_rows[...] = keys
@@ -102,9 +118,10 @@
         return 0
 
     lax.fori_loop(0, BLOCKS, rank_block, 0)
-    obl[0] = obl_in_ref[...]
+    obl[0] = obl_in_ref[...].astype(F32)
     pl.semaphore_wait(barrier, 2)
 
+    rows_in.wait()
     two_digits = digits[...].astype(BF16)
     for s in range(SUB):
         slots = lax.broadcasted_iota(jnp.int32, (ROWS, RB), 0) + s * ROWS
@@ -124,15 +141,17 @@
         found = (found[0:1, :] * 128.0 + found[1:2, :]).astype(jnp.int32)
         per = ROWS // RB
         for i in range(per):
-            auxs[0, s * per + i : s * per + i + 1, :] = found[:, i * RB : (i + 1) * RB]
+            now_aux[0, s * per + i : s * per + i + 1, :] = found[:, i * RB : (i + 1) * RB]
     starts = lax.broadcasted_iota(jnp.int32, (RB, RB), 1) * HALF
     total = jnp.zeros((RB, RB), jnp.int32)
     for j in range(BLOCKS):
         total += jnp.where(key_cols[j * RB : (j + 1) * RB, :] < starts, 1, 0)
     offsets = jnp.sum(total, axis=0, keepdims=True)
-    auxs[0, BLOCKS:, :] = jnp.broadcast_to(offsets, (8, RB))
+    offs[0] = offsets
+    auxs[0] = now_aux[0].astype(jnp.int16)
     for d in (0, 1):
         aux_copy(d, 0).start()
+        off_copy(d, 0).start()
     obl_copy(0).start()
     table_copy(0).start()
     table_copy(0).wait()
@@ -149,7 +168,7 @@
             return 0
 
         lax.fori_loop(0, PK // WIDTH, some, 0)
-        now_aux[i] = auxs[slot, :BLOCKS, :]
+        now_aux[i] = auxs[slot].astype(jnp.int32)
 
     def place_rows(slots, count, g, _):
         placed = []
@@ -163,7 +182,8 @@
                     ids = jnp.broadcast_to(ids, (16, RB)).astype(jnp.int16)
                     hit = jnp.where(slots16[...] == ids[None], jnp.ones((), BF16), jnp.zeros((), BF16))
                     hits.append(hit.reshape(HALF, RB))
-                packets.append(now[i, pl.ds(k * RB, WIN), :])
+                rows = lists.at[FAR] if len(slots) == 1 else now.at[i]
+                packets.append(rows[pl.ds(k * RB, WIN), :])
             found = packets[0] if len(packets) == 1 else jnp.concatenate(packets, axis=0)
             placed.append(
                 jnp.dot(jnp.concatenate(hits, axis=1), found, preferred_element_type=F32).astype(BF16)
@@ -204,11 +224,14 @@
         def _():
             for d in (0, 1):
                 aux_copy(d, t).wait_recv()
+                off_copy(d, t).wait_recv()
                 table_copy(place(d, t + 1)).start()
+            off_copy(0, t + 1).start()
             aux_copy(0, t + 1).start()
 
             @pl.when(t < FAR - 2)
             def _():
+                off_copy(1, t + 1).start()
                 aux_copy(1, t + 1).start()
 
             obl_copy(t).wait_recv()
@@ -219,15 +242,39 @@
         return 0
 
     lax.fori_loop(0, FAR, step, 0)
+
+    def sent(t, _):
+        for d in (0, 1):
+            for s in range(SUB):
+
+                @pl.when((t < FAR - 1) | ((s < SUB // 2) == (d == 0)))
+                def _(d=d, s=s):
+                    data_copy(d, t, s).wait_send()
+
+        for copy in (off_copy, aux_copy):
+            copy(0, t).wait_send()
+
+            @pl.when(t < FAR - 1)
+            def _(copy=copy):
+                copy(1, t).wait_send()
+
+        obl_copy(t).wait_send()
+        return 0
+
+    lax.fori_loop(0, FAR - 1, sent, 0)
+    for s in range(SUB // 2):
+        data_copy(0, FAR - 1, s).wait_recv()
+    off_copy(0, FAR - 1).wait_recv()
+    table_copy(FAR).start()
     aux_copy(0, FAR - 1).wait_recv()
-    table_copy(FAR).start()
-    for s in range(SUB):
-        data_copy(int(s >= SUB // 2), FAR - 1, s).wait_recv()
-    take(0, FAR)
+    now_aux[0] = auxs[FAR].astype(jnp.int32)
+    for s in range(SUB // 2, SUB):
+        data_copy(1, FAR - 1, s).wait_recv()
     table_copy(FAR).wait()
     lax.fori_loop(0, PANELS // ONE, functools.partial(place_rows, (FAR,), ONE), 0)
 
     obl_copy(FAR - 1).wait_recv()
+    wave_in.wait()
     w0, w1 = wave_ref[0], wave_ref[1]
 
     def filter_block(c, _):
@@ -253,7 +300,7 @@
             weights[pl.ds(k + RB, RB), right] = filt_re
         return 0
 
-    lax.fori_loop(0, BLOCKS, filter_block, 0)
+    lax.fori_loop(0, BLOCKS, filter_block, 0, unroll=4)
 
     tile = 512
 
@@ -269,38 +316,25 @@
 
     lax.fori_loop(0, HALF // tile, product, 0)
 
-    def sent(t, _):
-        for d in (0, 1):
-            for s in range(SUB):
-
-                @pl.when((t < FAR - 1) | ((s < SUB // 2) == (d == 0)))
-                def _(d=d, s=s):
-                    data_copy(d, t, s).wait_send()
-
-        aux_copy(0, t).wait_send()
-        obl_copy(t).wait_send()
-
-        @pl.when(t < FAR - 1)
-        def _():
-            aux_copy(1, t).wait_send()
-
-        return 0
-
-    lax.fori_loop(0, FAR, sent, 0)
+    sent(FAR - 1, 0)
 
 
 def on_device(packets, packet_bin, obliquity, wavelet):
-    vmem = pl.BlockSpec(memory_space=pltpu.VMEM)
+    vmem, hbm = pl.BlockSpec(memory_space=pltpu.VMEM), pl.BlockSpec(memory_space=pltpu.HBM)
     dma = pltpu.SemaphoreType.DMA
     return pl.pallas_call(
         kernel,
         out_shape=jax.ShapeDtypeStruct((2, HALF, WIDTH), F32),
-        in_specs=[vmem, vmem, vmem, pl.BlockSpec(memory_space=pltpu.SMEM)],
+        in_specs=[hbm, hbm, vmem, hbm],
         out_specs=vmem,
         scratch_shapes=[
+            pltpu.VMEM((PK, WIDTH), BF16),
+            pltpu.VMEM((BLOCKS, RB), jnp.int32),
+            pltpu.SMEM((2,), F32),
             pltpu.VMEM((GROUP, PK, WIDTH), BF16),
-            pltpu.VMEM((GROUP, 24, RB), jnp.int32),
-            pltpu.SMEM((GROUP, 8, RB), jnp.int32),
+            pltpu.VMEM((GROUP, BLOCKS, RB), jnp.int16),
+            pltpu.VMEM((GROUP, 1, RB), jnp.int32),
+            pltpu.SMEM((GROUP, 1, RB), jnp.int32),
             pltpu.VMEM((2, PK, WIDTH), BF16),
             pltpu.VMEM((2, BLOCKS, RB), jnp.int32),
             pltpu.VMEM((HALF, PANELS * WIDTH), BF16),
@@ -316,18 +350,21 @@
             dma((2, FAR, SUB)),
             dma((2, FAR)),
             dma((2, FAR)),
+            dma((2, FAR)),
+            dma((2, FAR)),
             dma((FAR,)),
             dma((FAR,)),
             dma((GROUP,)),
+            dma((3,)),
         ],
         compiler_params=pltpu.CompilerParams(
             collective_id=0, has_side_effects=True, vmem_limit_bytes=46 << 20
         ),
     )(
-        packets,
-        packet_bin.reshape(BLOCKS, RB),
-        obliquity.astype(F32).reshape(8, RB),
-        wavelet,
+        pltpu.with_memory_space_constraint(packets, pltpu.HBM),
+        pltpu.with_memory_space_constraint(packet_bin.reshape(BLOCKS, RB), pltpu.HBM),
+        pltpu.with_memory_space_constraint(obliquity.reshape(8, RB), pltpu.HBM),
+        pltpu.with_memory_space_constraint(wavelet, pltpu.HBM),
     )
 
 

time: 206 us -> 201 us (0.976)
  local copies, waits for them, and re-layouts: 3.9 us -> 1.32 us
    unnamed x7 -> x1, local copies, waits for them, and re-layouts: 3.9 us -> 1.32 us
where the time goes in v3:
time: 201 us
  Pallas kernels  200 us (100%)
    pallas_call x1, Pallas kernels, on_device(): pl.pallas_call(kernel, out_shape=jax.ShapeDtypeStruct((2, HALF, WIDTH), F...  200 us

profile of v3, /device:TPU:1, one launch (start us, length us, event | category | flops | bytes accessed | tf_op | source)
XLA Modules:
  0.0 201.3 jit_solution(11601139790213808198)
XLA Ops:
  0.0 200.0 %shard_map.46 = f32[2,1024,256]{2,1,0:T(8,128)S(1)} custom-call(bf16[2048,256]{1,0:T(8,128)(2,1)} %rows_hbm.1, s32[16,128]{1,0:T(8,128)} %bitcast.2, bf16[8,128]{1,0:T(8,128)(2,1)} %bitcast.3, f32[2]{0:T(128)} %wave_hbm.1), custom_call_target="tpu_custom_call" | custom-call | tf_op jit(solution)/shard_map/pallas_call | solution.py:325
  200.0 1.3 copy.6

commit v4 on v3

--- a/solution.py
+++ b/solution.py
@@ -26,8 +26,8 @@
 
 
 def kernel(rows_hbm, bins_hbm, obl_in_ref, wave_hbm, out_ref, rows_ref, bins_ref, wave_ref, lists, auxs, offs, tabs,
-           now, now_aux, panel, weights, slots16, onehot, key_cols, key_rows, rank_rows, digits, obl, send_sem,
-           recv_sem, aux_send, aux_recv, off_send, off_recv, obl_send, obl_recv, tab_sem, in_sem):
+           now, now_aux, panel, weights, slots16, key_cols, key_cols16, key_rows, rank_rows, digits, obl, send_sem,
+           recv_sem, aux_send, aux_recv, off_send, off_recv, obl_sem, tab_sem, in_sem):
     bins_in = pltpu.make_async_copy(bins_hbm, bins_ref, in_sem.at[0])
     rows_in = pltpu.make_async_copy(rows_hbm, rows_ref, in_sem.at[1])
     wave_in = pltpu.make_async_copy(wave_hbm, wave_ref, in_sem.at[2])
@@ -80,12 +80,12 @@
             device_id_type=MESH,
         )
 
-    def obl_copy(t):
+    def obl_copy(slot):
         return pltpu.make_async_remote_copy(
-            src_ref=obl.at[t],
-            dst_ref=obl.at[t + 1],
-            send_sem=obl_send.at[t],
-            recv_sem=obl_recv.at[t],
+            src_ref=obl.at[slot],
+            dst_ref=obl.at[1],
+            send_sem=obl_sem.at[0],
+            recv_sem=obl_sem.at[1],
             device_id=ahead[0],
             device_id_type=MESH,
         )
@@ -107,14 +107,17 @@
         lanes = slice(i * RB, (i + 1) * RB)
         digits[0:1, lanes] = high[i : i + 1, :]
         digits[1:2, lanes] = low[i : i + 1, :]
-        key_cols[i * RB : (i + 1) * RB, :] = jnp.broadcast_to(key_rows[i : i + 1, :], (RB, RB)).T
+        column = jnp.broadcast_to(key_rows[i : i + 1, :], (RB, RB)).T
+        key_cols[i * RB : (i + 1) * RB, :] = column
+        key_cols16[i * RB : (i + 1) * RB, :] = column.astype(jnp.int16)
 
     def rank_block(i, _):
-        mine = jnp.broadcast_to(key_rows[pl.ds(i, 1), :], (RB, RB))
-        total = jnp.zeros((RB, RB), jnp.int32)
+        mine = jnp.broadcast_to(key_rows[pl.ds(i, 1), :], (RB, RB)).astype(jnp.int16)
+        total = jnp.zeros((RB, RB), jnp.int16)
         for j in range(BLOCKS):
-            total += jnp.where(key_cols[j * RB : (j + 1) * RB, :] < mine, 1, 0)
-        rank_rows[pl.ds(i, 1), :] = jnp.sum(total, axis=0, keepdims=True)
+            less = key_cols16[j * RB : (j + 1) * RB, :] < mine
+            total += jnp.where(less, jnp.ones((), jnp.int16), jnp.zeros((), jnp.int16))
+        rank_rows[pl.ds(i, 1), :] = jnp.sum(total.astype(jnp.int32), axis=0, keepdims=True)
         return 0
 
     lax.fori_loop(0, BLOCKS, rank_block, 0)
@@ -122,6 +125,7 @@
     pl.semaphore_wait(barrier, 2)
 
     rows_in.wait()
+    onehot = panel.at[:ROWS, :PK]
     two_digits = digits[...].astype(BF16)
     for s in range(SUB):
         slots = lax.broadcasted_iota(jnp.int32, (ROWS, RB), 0) + s * ROWS
@@ -152,7 +156,11 @@
     for d in (0, 1):
         aux_copy(d, 0).start()
         off_copy(d, 0).start()
-    obl_copy(0).start()
+
+    @pl.when(rcv == FAR - 1)
+    def _():
+        obl_copy(0).start()
+
     table_copy(0).start()
     table_copy(0).wait()
 
@@ -170,27 +178,30 @@
         lax.fori_loop(0, PK // WIDTH, some, 0)
         now_aux[i] = auxs[slot].astype(jnp.int32)
 
-    def place_rows(slots, count, g, _):
-        placed = []
-        for j in [g * count + i for i in range(count)]:
-            b = jnp.where(j < BLOCKS, src * BLOCKS + j, (1 - src) * BLOCKS + rcv * 2 + j - BLOCKS)
-            hits, packets = [], []
-            for i, slot in enumerate(slots):
-                k = jnp.clip(tabs[slot, 0, b] // RB, 0, (PK - WIN) // RB)
-                for w in range(WIN // RB):
-                    ids = now_aux[i, pl.ds(k + w, 1), :] - b * HALF
-                    ids = jnp.broadcast_to(ids, (16, RB)).astype(jnp.int16)
-                    hit = jnp.where(slots16[...] == ids[None], jnp.ones((), BF16), jnp.zeros((), BF16))
-                    hits.append(hit.reshape(HALF, RB))
-                rows = lists.at[FAR] if len(slots) == 1 else now.at[i]
-                packets.append(rows[pl.ds(k * RB, WIN), :])
-            found = packets[0] if len(packets) == 1 else jnp.concatenate(packets, axis=0)
-            placed.append(
-                jnp.dot(jnp.concatenate(hits, axis=1), found, preferred_element_type=F32).astype(BF16)
-            )
-        lanes = pl.ds(pl.multiple_of(g * (count * WIDTH), count * WIDTH), count * WIDTH)
+    def found_rows(slots, j):
+        b = jnp.where(j < BLOCKS, src * BLOCKS + j, (1 - src) * BLOCKS + rcv * 2 + j - BLOCKS)
+        hits, packets = [], []
+        for i, slot in enumerate(slots):
+            k = jnp.clip(tabs[slot, 0, b] // RB, 0, (PK - WIN) // RB)
+            for w in range(WIN // RB):
+                ids = now_aux[i, pl.ds(k + w, 1), :] - b * HALF
+                ids = jnp.broadcast_to(ids, (16, RB)).astype(jnp.int16)
+                hit = jnp.where(slots16[...] == ids[None], jnp.ones((), BF16), jnp.zeros((), BF16))
+                hits.append(hit.reshape(HALF, RB))
+            rows = lists.at[FAR] if len(slots) == 1 else now.at[i]
+            packets.append(rows[pl.ds(k * RB, WIN), :])
+        found = packets[0] if len(packets) == 1 else jnp.concatenate(packets, axis=0)
+        return jnp.dot(jnp.concatenate(hits, axis=1), found, preferred_element_type=F32).astype(BF16)
+
+    def place_rows(slots, g, _):
+        placed = [found_rows(slots, g * PAIR + i) for i in range(PAIR)]
+        lanes = pl.ds(pl.multiple_of(g * (PAIR * WIDTH), PAIR * WIDTH), PAIR * WIDTH)
         panel[:, lanes] += jnp.concatenate(placed, axis=1)
         return 0
+
+    def place_far(buckets):
+        for j, rows in [(j, found_rows((FAR,), j)) for j in buckets]:
+            panel[:, pl.ds(pl.multiple_of(j * WIDTH, WIDTH), WIDTH)] += rows
 
     def step(t, _):
         slots = (t, place(1, t))
@@ -203,9 +214,7 @@
 
         def sub_block(s, _):
             groups = PANELS // PAIR
-            lax.fori_loop(
-                groups * s // SUB, groups * (s + 1) // SUB, functools.partial(place_rows, slots, PAIR), 0
-            )
+            lax.fori_loop(groups * s // SUB, groups * (s + 1) // SUB, functools.partial(place_rows, slots), 0)
 
             @pl.when(t < FAR - 1)
             def _():
@@ -234,8 +243,11 @@
                 off_copy(1, t + 1).start()
                 aux_copy(1, t + 1).start()
 
-            obl_copy(t).wait_recv()
-            obl_copy(t + 1).start()
+            @pl.when(rcv == t)
+            def _():
+                obl_copy(1).wait_recv()
+                obl_copy(1).start()
+
             for d in (0, 1):
                 table_copy(place(d, t + 1)).wait()
 
@@ -258,7 +270,6 @@
             def _(copy=copy):
                 copy(1, t).wait_send()
 
-        obl_copy(t).wait_send()
         return 0
 
     lax.fori_loop(0, FAR - 1, sent, 0)
@@ -271,13 +282,15 @@
     for s in range(SUB // 2, SUB):
         data_copy(1, FAR - 1, s).wait_recv()
     table_copy(FAR).wait()
-    lax.fori_loop(0, PANELS // ONE, functools.partial(place_rows, (FAR,), ONE), 0)
-
-    obl_copy(FAR - 1).wait_recv()
+
+    @pl.when(rcv == FAR - 1)
+    def _():
+        obl_copy(1).wait_recv()
+
     wave_in.wait()
     w0, w1 = wave_ref[0], wave_ref[1]
 
-    def filter_block(c, _):
+    def filter_block(c):
         here = c // (BLOCKS // 2) == src
         lane = jnp.where(here, rcv * 2 * WIDTH, BLOCKS * WIDTH)
         block = lax.rem(c, BLOCKS // 2)
@@ -285,7 +298,7 @@
             pl.ds(pl.multiple_of(block * RB, RB), RB),
             pl.ds(pl.multiple_of(lane, 2 * WIDTH), 2 * WIDTH),
         ].astype(F32)
-        row = obl[jnp.where(here, 0, FAR), pl.ds(block, 1), :]
+        row = obl[jnp.where(here, 0, 1), pl.ds(block, 1), :]
         scale = jnp.broadcast_to(row, (RB, RB)).T
         for i in range(2):
             re = data[:, i * WIDTH : i * WIDTH + RB]
@@ -298,9 +311,16 @@
             weights[pl.ds(k, RB), right] = filt_im
             weights[pl.ds(k + RB, RB), left] = -filt_im
             weights[pl.ds(k + RB, RB), right] = filt_re
-        return 0
-
-    lax.fori_loop(0, BLOCKS, filter_block, 0, unroll=4)
+
+    place_far([BLOCKS, BLOCKS + 1] + [lax.rem(rcv * 2 + i, BLOCKS) for i in range(ONE - 2)])
+
+    def far_and_filter(g, _):
+        for i in range(BLOCKS // 2):
+            filter_block(g * (BLOCKS // 2) + i)
+        place_far([lax.rem(rcv * 2 + (g + 1) * ONE - 2 + i, BLOCKS) for i in range(ONE)])
+        return 0
+
+    lax.fori_loop(0, PANELS // ONE - 1, far_and_filter, 0)
 
     tile = 512
 
@@ -317,6 +337,7 @@
     lax.fori_loop(0, HALF // tile, product, 0)
 
     sent(FAR - 1, 0)
+    obl_copy(0).wait_send()
 
 
 def on_device(packets, packet_bin, obliquity, wavelet):
@@ -340,25 +361,24 @@
             pltpu.VMEM((HALF, PANELS * WIDTH), BF16),
             pltpu.VMEM((BLOCKS * WIDTH, 2 * WIDTH), BF16),
             pltpu.VMEM((HALF // 16, 16, RB), jnp.int16),
-            pltpu.VMEM((ROWS, PK), BF16),
             pltpu.VMEM((PK, RB), jnp.int32),
+            pltpu.VMEM((PK, RB), jnp.int16),
             pltpu.VMEM((BLOCKS, RB), jnp.int32),
             pltpu.VMEM((BLOCKS, RB), jnp.int32),
             pltpu.VMEM((8, PK), F32),
-            pltpu.VMEM((FAR + 1, 8, RB), F32),
+            pltpu.VMEM((2, 8, RB), F32),
             dma((2, FAR, SUB)),
             dma((2, FAR, SUB)),
             dma((2, FAR)),
             dma((2, FAR)),
             dma((2, FAR)),
             dma((2, FAR)),
-            dma((FAR,)),
-            dma((FAR,)),
+            dma((2,)),
             dma((GROUP,)),
             dma((3,)),
         ],
         compiler_params=pltpu.CompilerParams(
-            collective_id=0, has_side_effects=True, vmem_limit_bytes=46 << 20
+            collective_id=0, has_side_effects=True, vmem_limit_bytes=48 << 20
         ),
     )(
         pltpu.with_memory_space_constraint(packets, pltpu.HBM),

time: 201 us -> 201 us (level)
  no operation moved by 1% of the time
where the time goes in v4:
time: 201 us
  Pallas kernels  200 us (100%)
    pallas_call x1, Pallas kernels, on_device(): pl.pallas_call(kernel, out_shape=jax.ShapeDtypeStruct((2, HALF, WIDTH), F...  200 us

profile of v4, /device:TPU:1, one launch (start us, length us, event | category | flops | bytes accessed | tf_op | source)
XLA Modules:
  0.0 201.0 jit_solution(15999476051067288122)
XLA Ops:
  0.0 199.7 %shard_map.46 = f32[2,1024,256]{2,1,0:T(8,128)S(1)} custom-call(bf16[2048,256]{1,0:T(8,128)(2,1)} %rows_hbm.1, s32[16,128]{1,0:T(8,128)} %bitcast.2, bf16[8,128]{1,0:T(8,128)(2,1)} %bitcast.3, f32[2]{0:T(128)} %wave_hbm.1), custom_call_target="tpu_custom_call" | custom-call | tf_op jit(solution)/shard_map/pallas_call | solution.py:346
  199.7 1.3 copy.6

commit v5 on v4

--- a/solution.py
+++ b/solution.py
@@ -203,6 +203,23 @@
         for j, rows in [(j, found_rows((FAR,), j)) for j in buckets]:
             panel[:, pl.ds(pl.multiple_of(j * WIDTH, WIDTH), WIDTH)] += rows
 
+    def sent(t, _):
+        for d in (0, 1):
+            for s in range(SUB):
+
+                @pl.when((t < FAR - 1) | ((s < SUB // 2) == (d == 0)))
+                def _(d=d, s=s):
+                    data_copy(d, t, s).wait_send()
+
+        for copy in (off_copy, aux_copy):
+            copy(0, t).wait_send()
+
+            @pl.when(t < FAR - 1)
+            def _(copy=copy):
+                copy(1, t).wait_send()
+
+        return 0
+
     def step(t, _):
         slots = (t, place(1, t))
         take(0, slots[0])
@@ -228,6 +245,10 @@
             return 0
 
         lax.fori_loop(0, SUB, sub_block, 0)
+
+        @pl.when((t > 0) & (t < FAR - 1))
+        def _():
+            sent(t - 1, 0)
 
         @pl.when(t < FAR - 1)
         def _():
@@ -255,24 +276,6 @@
 
     lax.fori_loop(0, FAR, step, 0)
 
-    def sent(t, _):
-        for d in (0, 1):
-            for s in range(SUB):
-
-                @pl.when((t < FAR - 1) | ((s < SUB // 2) == (d == 0)))
-                def _(d=d, s=s):
-                    data_copy(d, t, s).wait_send()
-
-        for copy in (off_copy, aux_copy):
-            copy(0, t).wait_send()
-
-            @pl.when(t < FAR - 1)
-            def _(copy=copy):
-                copy(1, t).wait_send()
-
-        return 0
-
-    lax.fori_loop(0, FAR - 1, sent, 0)
     for s in range(SUB // 2):
         data_copy(0, FAR - 1, s).wait_recv()
     off_copy(0, FAR - 1).wait_recv()
@@ -336,7 +339,7 @@
 
     lax.fori_loop(0, HALF // tile, product, 0)
 
-    sent(FAR - 1, 0)
+    lax.fori_loop(FAR - 2, FAR, sent, 0)
     obl_copy(0).wait_send()
 
 

time: 201 us -> 201 us (level)
  no operation moved by 1% of the time
where the time goes in v5:
time: 201 us
  Pallas kernels  200 us (100%)
    pallas_call x1, Pallas kernels, on_device(): pl.pallas_call(kernel, out_shape=jax.ShapeDtypeStruct((2, HALF, WIDTH), F...  200 us

profile of v5, /device:TPU:1, one launch (start us, length us, event | category | flops | bytes accessed | tf_op | source)
XLA Modules:
  0.0 201.1 jit_solution(16901155695801806832)
XLA Ops:
  0.0 199.7 %shard_map.46 = f32[2,1024,256]{2,1,0:T(8,128)S(1)} custom-call(bf16[2048,256]{1,0:T(8,128)(2,1)} %rows_hbm.1, s32[16,128]{1,0:T(8,128)} %bitcast.2, bf16[8,128]{1,0:T(8,128)(2,1)} %bitcast.3, f32[2]{0:T(128)} %wave_hbm.1), custom_call_target="tpu_custom_call" | custom-call | tf_op jit(solution)/shard_map/pallas_call | solution.py:349
  199.7 1.3 copy.6
